TPU v7x, 128 devices: a whole 4x4x4 slice. The times are simulated.
128 devices in a mesh: front: 16 (over z, y), blk: 8 (over x, core).
Axes of the slice: x: 4, y: 4, z: 4, core: 2. Of those that a mesh axis runs over, the one named last changes fastest.
Arguments:
- contribution: bfloat16 [16, 8192, 8192], P('front', 'blk'), may hold values from -0.0625 to 0.0625
- omega_cols: bfloat16 [16, 8192, 256], P('front', 'blk'), may hold values from -6 to 6
- psi_cols: bfloat16 [16, 8192, 256], P('front', 'blk'), may hold values from -6 to 6
- lengths: int32 [16], P('front'), may hold values from 1024 to 8192, as said below
- selectors: int32 [16, 64], P('front', 'blk'), may hold values from 0 to 15, as said below
- assign: int32 [16, 1], replicated, may hold values from 0 to 3
- pivot_block: float32 [4, 256, 256], replicated, as said below
Outputs:
- row_panel: float32 [8, 2048, 4, 256], P('blk', 'front')
- col_panel: float32 [8, 2048, 4, 256], P('blk', 'front')
Inputs may be any that keep to these rules, and one draw needn't show every extreme that they name: `lengths`: the largest length equals 8192. `selectors`: for one child and one row block the values are distinct. `assign`: every parent has at least one child. `pivot_block`: symmetric, each diagonal entry exceeds the sum of magnitudes of the rest of its row.
All inputs are finite; a program needn't handle non-finite values.
Results may differ from a plain program's by a relative error of at most 0.0003.
Values may be sent and summed in bfloat16 or wider, within the bound.
A program may use at most 128 MiB of HBM per device.

v0:
```python
import jax
import jax.numpy as jnp
from jax import lax
from jax.sharding import PartitionSpec as P


def extend_rows(samples, chosen):
    sub_count = chosen.shape[0]
    sample_width = samples.shape[-1]
    sub_blocks = samples.reshape(2, sub_count, -1, sample_width)
    placed = jnp.zeros((2, 2 * sub_count, sub_blocks.shape[2], sample_width), samples.dtype)
    placed = placed.at[:, chosen].set(sub_blocks)
    return placed.reshape(2, -1, sample_width)


def on_device(contribution, omega_cols, psi_cols, lengths, selectors, assign, pivot_block):
    front_block = contribution[0]
    omega_local = omega_cols[0]
    psi_local = psi_cols[0]
    length = lengths[0]
    chosen = selectors[0]
    local_rows = front_block.shape[0]
    sample_width = omega_local.shape[1]
    parent_count = pivot_block.shape[0]
    row_offset = lax.axis_index("blk") * local_rows
    live_rows = row_offset + jnp.arange(local_rows, dtype=jnp.int32) < length
    shard_rows = lax.all_gather(omega_local, "blk", axis=0, tiled=True)
    shard_live = jnp.arange(shard_rows.shape[0], dtype=jnp.int32) < length
    shard_rows = jnp.where(shard_live[:, None], shard_rows, jnp.zeros_like(shard_rows))
    block_cols = front_block
    row_sample = jnp.dot(block_cols, shard_rows, preferred_element_type=jnp.float32)
    psi_live = jnp.where(live_rows[:, None], psi_local, jnp.zeros_like(psi_local))
    block_cols = front_block
    col_sample = lax.psum_scatter(
        lax.dot_general(
            block_cols, psi_live, (((0,), (0,)), ((), ())), preferred_element_type=jnp.float32
        ),
        "blk",
        scatter_dimension=0,
        tiled=True,
    )
    stacked = jnp.stack([row_sample, col_sample])
    stacked = jnp.where(live_rows[None, :, None], stacked, jnp.zeros_like(stacked))
    extended = extend_rows(stacked, chosen)
    parent_ids = jnp.arange(parent_count, dtype=jnp.int32)
    slice_rows = extended.shape[1] // lax.axis_size("front")
    own_parent = lax.dynamic_slice_in_dim(assign[:, 0], lax.axis_index("front"), 1, 0)
    parent_mask = (own_parent == parent_ids)[None, None, :, None]
    slab_rows = jnp.transpose(extended, (1, 0, 2))[:, :, None, :]
    summed = lax.psum_scatter(
        jnp.where(parent_mask, slab_rows, jnp.zeros_like(slab_rows)),
        "front",
        scatter_dimension=0,
        tiled=True,
    )
    factor = jnp.linalg.cholesky(pivot_block)
    sample_rows = summed.reshape(-1, parent_count, sample_width)
    right_sides = jnp.transpose(sample_rows, (1, 2, 0))
    solved = jax.scipy.linalg.solve_triangular(factor, right_sides, lower=True)
    solved = jnp.transpose(solved, (2, 0, 1)).reshape(slice_rows, 2, parent_count, sample_width)
    row_panel = solved[:, 0][None]
    col_panel = solved[:, 1][None]
    return (row_panel, col_panel)


def solution(mesh):
    in_specs = (
        P("front", "blk", None),
        P("front", "blk", None),
        P("front", "blk", None),
        P("front"),
        P("front", "blk"),
        P(),
        P(),
    )
    out_specs = (P("blk", "front", None, None), P("blk", "front", None, None))
    return jax.shard_map(
        on_device, mesh=mesh, in_specs=in_specs, out_specs=out_specs, check_vma=False
    )
```

profile of v0, /device:TPU:1, one launch (start us, length us, event | category | flops | bytes accessed | tf_op | source)
XLA Modules:
  0.0 362.1 jit_solution(12689946792835524039)
XLA Ops:
  7.2 0.0 copy-start
  7.2 0.0 all-gather.3.cloned.1.call-start
  7.2 0.7 all-gather.3.cloned.1.call-update
  7.9 0.0 reduce-scatter.2.cloned.1.call-start
  8.6 13.9 %fusion.4 = f32[8192,256]{0,1:T(8,128)} fusion(bf16[1,1024,8192]{2,1,0:T(8,128)(2,1)} %param.7, bf16[1,1024,256]{2,1,0:T(8,128)(2,1)} %param.9, pred[1024]{0:T(1024)(128)(4,1)S(1)} %add_compare_fusion), kind=kOutput, calls=%fused_computation.7 | convolution fusion | flops 4295229440 | bytes 25691136 | tf_op jit(solution)/shard_map/dot_general | solution.py:35
  22.5 0.0 reduce-scatter.2.cloned.1.call-update
  22.5 0.2 all-reduce.4.cloned.1.call-start
  22.8 0.6 constant_dynamic-slice_fusion.1
  23.3 0.6 iota_compare_fusion.4
  24.0 21.5 %all-gather.3.cloned.1.call-done = bf16[1,8192,256]{2,1,0:T(8,128)(2,1)} async-done(((bf16[1,1024,256]{2,1,0:T(8,128)(2,1)}), bf16[1,8192,256]{2,1,0:T(8,128)(2,1)}) %all-gather.3.cloned.1.call-update) | async-done | bytes 4194320 | tf_op jit(solution)/shard_map/all_gather | solution.py:27
  45.5 10.3 %fusion.10 = f32[1024,256]{0,1:T(8,128)S(1)} fusion(bf16[1,1024,8192]{2,1,0:T(8,128)(2,1)} %param.7, bf16[1,8192,256]{2,1,0:T(8,128)(2,1)} %all-gather.3.cloned.1.call-done, pred[8192]{0:T(1024)(128)(4,1)S(1)} %iota_compare_fusion.3), kind=kOutput, calls=%fused_computation.14 | convolution fusion | flops 4297064448 | bytes 22028288 | tf_op jit(solution)/shard_map/dot_general | solution.py:31
  55.8 0.3 copy.53
  56.2 43.2 %reduce-scatter.2.cloned.1.call-done = f32[1024,256]{0,1:T(8,128)} async-done(((f32[8192,256]{0,1:T(8,128)}), f32[1024,256]{0,1:T(8,128)}) %reduce-scatter.2.cloned.1.call-update) | async-done | bytes 1048592 | tf_op jit(solution)/shard_map/reduce_scatter | solution.py:34
  99.3 2.5 copy.54
  101.9 1.5 fusion.8
  103.4 2.4 broadcast_in_dim.72
  105.8 3.6 scatter_fusion
  109.4 7.8 %copy.45 = f32[2048,2,256]{2,1,0:T(2,128)S(1)} copy(f32[2048,2,256]{2,0,1:T(8,128)} %bitcast.83) | data formatting | bytes 8388608 | tf_op jit(solution)/shard_map/transpose | solution.py:49
  117.2 8.1 %broadcast_select_fusion = f32[2048,2,4,256]{3,2,1,0:T(4,128)} fusion(f32[2048,2,256]{2,1,0:T(2,128)S(1)} %copy.45, pred[4]{0:T(512)(128)(4,1)S(1)} %iota_compare_fusion.4), kind=kLoop, calls=%fused_computation.8 | loop fusion | flops 4194304 | bytes 20971524 | tf_op jit(solution)/shard_map/jit(_where)/select_n | solution.py:51
  125.2 0.0 all-reduce.4.cloned.1.call-update
  125.3 0.6 copy-done.4
  125.9 0.6 dynamic-slice.5
  127.1 0.3 copy.39
  127.4 0.1 fusion.13
  127.6 46.9 %custom-call.17 = f32[4,128,128]{2,1,0:T(8,128)S(1)} custom-call(f32[4,128,128]{2,1,0:T(8,128)S(1)} %cholesky.122), custom_call_target="Cholesky" | custom-call | tf_op jit(solution)/shard_map/jit(cholesky)/cholesky | solution.py:56
  174.5 0.1 cholesky.117
  174.7 39.5 %custom-call.18 = f32[4,1,128,128]{2,3,1,0:T(8,128)S(1)} custom-call(f32[4,1,128,128]{3,2,1,0:T(8,128)S(1)} %select_bitcast_fusion), custom_call_target="InvertDiagBlocksLowerTriangular" | custom-call | tf_op jit(solution)/shard_map/jit(cholesky)/cholesky | solution.py:56
  214.2 0.4 constant_dynamic-update-slice_fusion.1
  214.6 0.7 convolution_subtract_fusion.1
  215.3 46.9 %custom-call.19 = f32[4,128,128]{2,1,0:T(8,128)S(1)} custom-call(f32[4,128,128]{2,1,0:T(8,128)S(1)} %convolution_subtract_fusion.1), custom_call_target="Cholesky" | custom-call | tf_op jit(solution)/shard_map/jit(cholesky)/cholesky | solution.py:56
  262.2 0.1 select_reduce_fusion
  262.3 0.1 compare_reduce_fusion
  262.5 0.2 select_select_fusion
  262.7 0.1 triangular_solve.62
  262.7 5.5 %while.1 = (s32[]{:T(128)}, f32[4,256,256]{2,1,0:T(8,128)S(1)}, s32[2,2]{1,0:T(2,128)S(1)}, f32[2,4,128,128]{3,2,0,1:T(8,128)}, s32[]{:T(128)}) while((s32[]{:T(128)}, f32[4,256,256]{2,1,0:T(8,128)S(1)}, s32[2,2]{1,0:T(2,128)S(1)}, f32[2,4,128,128]{3,2,0,1:T(8,128)}, s32[]{:T(128)}) %tuple.28), condition=%wide.while_cond, body=%wide.while_body.sunk | while | flops 2 | bytes 525421 | solution.py:59
  262.8 0.6 fusion.34
  263.4 2.1 bitcast_dynamic-update-slice_fusion.2
  265.5 0.6 fusion.34
  266.1 2.1 bitcast_dynamic-update-slice_fusion.2
  268.3 80.1 %custom-call.20 = f32[4,2,128,128]{2,3,1,0:T(8,128)} custom-call(f32[4,2,128,128]{3,2,1,0:T(8,128)} %bitcast.90), custom_call_target="InvertDiagBlocksLowerTriangular" | custom-call | tf_op jit(solution)/shard_map/jit(_solve_triangular)/vmap()/triangular_solve | solution.py:59
  348.3 1.3 constant_dynamic-slice_fusion.2
  349.7 0.4 copy.46
  350.1 1.6 fusion.14
  351.7 0.6 convolution_subtract_fusion
  352.3 1.6 fusion.20
  353.9 0.1 maximum_bitcast_fusion
  354.0 0.4 copy.49
  354.4 1.1 slice_bitcast_fusion
  (23 shorter events, 0.2 us)
Async XLA Ops:
  7.2 15.6 %copy-start = (s32[16,1]{0,1:T(1,128)S(1)}, s32[16,1]{0,1:T(1,128)}, u32[]{:S(2)}) copy-start(s32[16,1]{0,1:T(1,128)} %param.12) | copy-start | bytes 196
  7.2 38.3 %all-gather.3.cloned.1.call-start = ((), (), s32[]{:S(2)}) async-start(), calls=%async_computation.2 | async-start | bytes 4718592 | tf_op jit(solution)/shard_map/all_gather | solution.py:27
  7.9 91.4 %reduce-scatter.2.cloned.1.call-start = ((), (), s32[]{:S(2)}) async-start(), calls=%async_computation.1 | async-start | bytes 9437184 | tf_op jit(solution)/shard_map/reduce_scatter | solution.py:34
  22.5 1.4 copy-start.3
  22.5 325.8 %all-reduce.4.cloned.1.call-start = ((), (), s32[]{:S(2)}) async-start(), calls=%async_computation.3 | async-start | bytes 33554432
  125.2 0.7 copy-start.4
  125.2 1.9 copy-start.2
  351.7 3.9 %copy-start.1 = (s32[16,1]{0,1:T(1,128)S(1)}, s32[16,1]{0,1:T(1,128)}, u32[]{:S(2)}) copy-start(s32[16,1]{0,1:T(1,128)} %param.12) | copy-start | bytes 196
Sparse Core Ops, SparseCore 0:
  9.7 35.6 all-gather.2
  47.9 51.4 reduce-scatter.1
  125.4 221.0 all-reduce.3
where the time goes:
time: 363 us; the launch traced here: 362 us
  other arithmetic  224 us (62%)
  waiting for transfers between devices  65.4 us (18%)
  matrix products  29.1 us (8%)
  local copies, waits for them, and re-layouts  27.8 us (8%)
  between operations  15.3 us (4%)
    another operation x9, other arithmetic, on_device(): factor = jnp.linalg.cholesky(pivot_block)  134 us
    another operation x4, other arithmetic, on_device(): solved = jax.scipy.linalg.solve_triangular(factor, right_sides, lower=True)  80.3 us
    reduce_scatter x1, waiting for transfers between devices, on_device(): lax.psum_scatter(lax.dot_general(block_cols, psi_live, (((0,), (0,)), (()...  43.2 us
    all_gather x1, waiting for transfers between devices, on_device(): shard_rows = lax.all_gather(omega_local, 'blk', axis=0, tiled=True)  21.5 us
    dot_general x1, matrix products, on_device(): lax.dot_general(block_cols, psi_live, (((0,), (0,)), ((), ())), preferred...  13.9 us
    dot_general x1, matrix products, on_device(): jnp.dot(block_cols, shard_rows, preferred_element_type=jnp.float32)  10.3 us
    select_n x1, other arithmetic, on_device(): jnp.where(parent_mask, slab_rows, jnp.zeros_like(slab_rows))  8.06 us
    transpose x1, local copies, waits for them, and re-layouts, on_device(): slab_rows = jnp.transpose(extended, (1, 0, 2))[:, :, None, :]  7.78 us
  transfers between devices with their start and end apart: 3, of which 2 were waited for; matrix products, arithmetic and copies ran while one was open for 68% of the time, Pallas kernels for 0%

commit v1 on v0

v1 whole, which is shorter than its diff:
```python
import functools

import jax
import jax.numpy as jnp
from jax import lax
from jax.experimental import pallas as pl
from jax.experimental.pallas import tpu as pltpu
from jax.sharding import PartitionSpec as P

MESH = pl.DeviceIdType.MESH
HI = lax.Precision.HIGHEST
F32 = jnp.float32
I32 = jnp.int32
BF16 = jnp.bfloat16
NB = 64
TOP = 32766.0


def join16(t, axis):
    half = t.shape[axis] // 2
    low = lax.slice_in_dim(t, 0, half, axis=axis)
    high = lax.slice_in_dim(t, half, 2 * half, axis=axis)
    return (high << 16) | (low & 0xFFFF)


def scale_of(v):
    m = jnp.max(jnp.abs(v), axis=0, keepdims=True)
    e = jnp.floor(jnp.log2(jnp.maximum(m, 2.0**-100))) + 1.0
    return e, jnp.exp2(-e) * TOP


def encode_lanes(v):
    e, factor = scale_of(v)
    q = jnp.round(v * factor).astype(I32)
    ex = join16(e.astype(I32), 1)
    return join16(q, 1), jnp.broadcast_to(ex, (8, ex.shape[1]))


def encode_rows(v):
    e, factor = scale_of(v)
    q = jnp.round(v * factor).astype(I32)
    return join16(q, 0), jnp.broadcast_to(e.astype(I32), (8, v.shape[1]))


def low16(t):
    return (t << 16) >> 16


def high16(t):
    return t >> 16


def unscale(e):
    return jnp.exp2(e.astype(F32)) * (1.0 / TOP)


def decode_lanes(ref, rows):
    ex = ref[rows : rows + 1, :]
    q = ref[0:rows, :]
    low = low16(q).astype(F32) * unscale(low16(ex))
    high = high16(q).astype(F32) * unscale(high16(ex))
    return jnp.concatenate([low, high], axis=1)


def factor_block(w, blk):
    n = w.shape[0]
    o = blk * NB
    r8 = lax.broadcasted_iota(I32, (8, 128), 0)
    wb = w[o : o + NB, :]
    wide = wb.shape[1] // 128
    tile = lambda f: jnp.concatenate([f] * wide, axis=1)
    strips = [wb[8 * s : 8 * s + 8, :] for s in range(NB // 8)]
    for s in range(NB // 8):
        so = o + 8 * s
        left = NB // 8 - s
        cols = [
            [jnp.broadcast_to(strips[t][:, so + k : so + k + 1], (8, 128)) for k in range(8)]
            for t in range(s, NB // 8)
        ]
        st = strips[s]
        scale = jnp.zeros((8, 128), F32)
        fs = [[None] * 8 for _ in range(left)]
        for k in range(8):
            pivot = jnp.broadcast_to(cols[0][k][k : k + 1, :], (8, 128))
            inverse = 1.0 / pivot
            scale = jnp.where(r8 == k, lax.rsqrt(pivot), scale)
            for t in range(left):
                f = cols[t][k] * inverse
                fs[t][k] = jnp.where(r8 > k, f, 0.0) if t == 0 else f
            for j in range(k + 1, 8):
                u = jnp.broadcast_to(cols[0][j][k : k + 1, :], (8, 128))
                for t in range(left):
                    cols[t][j] = cols[t][j] - fs[t][k] * u
        for k in range(8):
            st = st - tile(fs[0][k]) * jnp.broadcast_to(st[k : k + 1, :], st.shape)
        for t in range(1, left):
            acc = strips[s + t]
            for k in range(8):
                acc = acc - tile(fs[t][k]) * jnp.broadcast_to(st[k : k + 1, :], st.shape)
            strips[s + t] = acc
        strips[s] = st
        w[so : so + 8, :] = st * tile(scale)
    if o + NB < n:
        y = w[o : o + NB, :]
        later = y[:, o + NB : n]
        w[o + NB : n, :] = w[o + NB : n, :] - lax.dot_general(
            later, y, (((0,), (0,)), ((), ())), precision=HI, preferred_element_type=F32
        )


def kernel(
    front_ref, omega_ref, psi_ref, length_ref, chosen_ref, assign_ref, pivot_ref,
    row_ref, col_ref,
    cbuf, ombuf, raw, psit, pivots, w, mt, psend, pown, precv, racc, sfin,
    xsend, xrecv, rq, rslot, rrecv, cq, cslot, crecv,
    csem, insem, om_send, om_recv, p_send, p_recv, x_send, x_recv, r_send, r_recv, c_send, c_recv,
):
    f = lax.axis_index("front")
    b = lax.axis_index("blk")
    X = b // 2
    c = lax.rem(b, 2)
    rows = 1024
    half = rows // 2
    blk_at = lambda dx, core: lax.rem(X + dx, 4) * 2 + core
    right = {"blk": blk_at(1, c)}
    left = {"blk": blk_at(3, c)}
    partner = {"blk": blk_at(0, 1 - c)}
    z, y = f // 4, lax.rem(f, 4)
    offs = [(dz, dy) for dz in range(4) for dy in range(4)][1:]
    front_at = lambda dz, dy: lax.rem(z + dz, 4) * 4 + lax.rem(y + dy, 4)

    barrier = pltpu.get_barrier_semaphore()
    peers = [right, left, partner] + [{"front": front_at(*o)} for o in offs]
    for peer in peers:
        pl.semaphore_signal(barrier, inc=1, device_id=peer, device_id_type=MESH)

    omega_in = pltpu.make_async_copy(omega_ref.at[0], raw.at[0], insem.at[0])
    psi_in = pltpu.make_async_copy(psi_ref.at[0], raw.at[1], insem.at[1])
    pivot_in = pltpu.make_async_copy(pivot_ref, pivots, insem.at[2])
    omega_in.start()
    psi_in.start()

    def chunk_in(dx, core):
        j = blk_at(dx, core)
        return pltpu.make_async_copy(
            front_ref.at[0, :, pl.ds(pl.multiple_of(j * rows, rows), rows)], cbuf.at[j], csem.at[j]
        )

    for k in range(4):
        chunk_in((k + 2) % 4, 1 - c).start()
        chunk_in((k + 2) % 4, c).start()
    pivot_in.start()

    length = length_ref[0]
    live = lax.broadcasted_iota(I32, (rows, 256), 0) + b * rows < length

    omega_in.wait()
    ombuf[b] = jnp.where(live, raw[0].astype(F32), 0.0).astype(BF16)
    pl.semaphore_wait(barrier, len(peers))

    def piece(blk, h, sem, to):
        ref = ombuf.at[blk, pl.ds(h * half, half)]
        return pltpu.make_async_remote_copy(
            src_ref=ref, dst_ref=ref, send_sem=om_send.at[sem], recv_sem=om_recv.at[sem],
            device_id=to, device_id_type=MESH,
        )

    own_right = [piece(b, h, h, right) for h in range(2)]
    own_left = [piece(b, h, 2 + h, left) for h in range(2)]
    own_right[0].start()
    own_left[1].start()
    own_right[1].start()
    own_left[0].start()
    cross = {}

    def cross_send(dx, h):
        cp = piece(blk_at(dx, c), h, 6 + dx * 2 + h, partner)
        cp.start()
        cross[dx, h] = cp

    cross_send(0, 0)
    cross_send(0, 1)

    psi_in.wait()
    psit[...] = jnp.where(live, raw[1].astype(F32), 0.0).T.astype(BF16)

    def partial_to_partner(dx):
        return pltpu.make_async_remote_copy(
            src_ref=psend.at[dx], dst_ref=precv.at[dx], send_sem=p_send.at[dx], recv_sem=p_recv.at[dx],
            device_id=partner, device_id_type=MESH,
        )

    @pl.loop(0, 4)
    def _(k):
        dx = lax.rem(k + 2, 4)
        chunk_in(dx, 1 - c).wait()
        psend[dx] = jnp.dot(psit[...], cbuf[blk_at(dx, 1 - c)], preferred_element_type=F32)
        partial_to_partner(dx).start()
        chunk_in(dx, c).wait()
        pown[dx] = jnp.dot(psit[...], cbuf[blk_at(dx, c)], preferred_element_type=F32)

    def row_add(dx, core, h, first=False):
        blk = blk_at(dx, core)
        t = jnp.dot(
            cbuf[blk, :, h * half : (h + 1) * half], ombuf[blk, h * half : (h + 1) * half, :],
            preferred_element_type=F32,
        )
        racc[...] = t if first else racc[...] + t

    row_add(0, c, 0, True)
    row_add(0, c, 1)
    for h in range(2):
        cross[0, h].wait_recv()
        row_add(0, 1 - c, h)

    own_right[0].wait_recv()
    fwd_right = piece(blk_at(3, c), 0, 4, right)
    fwd_right.start()
    cross_send(3, 0)
    own_left[1].wait_recv()
    fwd_left = piece(blk_at(1, c), 1, 5, left)
    fwd_left.start()
    cross_send(1, 1)

    pivot_in.wait()
    parent = assign_ref[f, 0]
    w[:, 0:256] = pivots[parent]
    eye = lax.broadcasted_iota(I32, (256, 256), 0) == lax.broadcasted_iota(I32, (256, 256), 1)
    w[:, 256:512] = jnp.where(eye, 1.0, 0.0)
    factor_block(w, 0)
    factor_block(w, 1)

    for dx, h in ((3, 0), (1, 1)):
        row_add(dx, c, h)
        cross[dx, h].wait_recv()
        row_add(dx, 1 - c, h)

    own_right[1].wait_recv()
    cross_send(3, 1)
    own_left[0].wait_recv()
    cross_send(1, 0)

    factor_block(w, 2)
    factor_block(w, 3)
    mt[...] = w[:, 256:512].T

    for dx, h in ((3, 1), (1, 0)):
        row_add(dx, c, h)
        cross[dx, h].wait_recv()
        row_add(dx, 1 - c, h)

    for dx in (2, 1, 3, 0):
        partial_to_partner(dx).wait_recv()
        pown[dx] = pown[dx] + precv[dx]

    def ring(sem, to):
        return pltpu.make_async_remote_copy(
            src_ref=xsend.at[sem], dst_ref=xrecv.at[sem], send_sem=x_send.at[sem], recv_sem=x_recv.at[sem],
            device_id=to, device_id_type=MESH,
        )

    def ring_put(sem, v):
        q, e = encode_lanes(v)
        xsend[sem, 0:128, :] = q
        xsend[sem, 128:136, :] = e

    ring_get = lambda sem: decode_lanes(xrecv.at[sem], 128)
    part = lambda dx, g, h: pown[dx, g * 128 : (g + 1) * 128, h * half : (h + 1) * half]
    R1, R2, R3, L1, L2, L3 = 0, 2, 4, 6, 8, 10
    for g in range(2):
        ring_put(R1 + g, part(2, g, 0))
        ring_put(L1 + g, part(2, g, 1))

    fwd_right.wait_recv()
    cross_send(2, 0)
    fwd_left.wait_recv()
    cross_send(2, 1)
    copies = {}

    def ring_send(sem, to):
        copies[sem] = ring(sem, to)
        copies[sem].start()

    for g in range(2):
        ring_send(R1 + g, right)
        ring_send(L1 + g, left)
    row_add(2, c, 0)
    row_add(2, c, 1)
    for h in range(2):
        cross[2, h].wait_recv()
        row_add(2, 1 - c, h)

    sub_live = lax.broadcasted_iota(I32, (128, 256), 0) + b * rows
    for k in range(8):
        s = jnp.where(sub_live + k * 128 < length, racc[k * 128 : (k + 1) * 128, :], 0.0)
        zk = jnp.dot(s, mt[...], precision=HI, preferred_element_type=F32)
        q, e = encode_lanes(zk)
        rq[k, 0:128, :] = q
        rq[k, 128:136, :] = e
    rq[8] = jnp.zeros(rq.shape[1:], I32)
    for g in range(2):
        cq[g, 8] = jnp.zeros(cq.shape[2:], I32)
    source = []
    for m in range(16):
        at = jnp.int32(8)
        for k in range(8):
            at = jnp.where(chosen_ref[0, k] == m, jnp.int32(k), at)
        source.append(at)
    for m in range(16):
        rslot[m] = rq[source[m]]
    rsends = []
    for i, o in enumerate(offs):
        cp = pltpu.make_async_remote_copy(
            src_ref=rslot.at[front_at(*o)], dst_ref=rrecv.at[f], send_sem=r_send.at[i], recv_sem=r_recv.at[i],
            device_id={"front": front_at(*o)}, device_id_type=MESH,
        )
        cp.start()
        rsends.append(cp)
    rrecv[f] = rslot[f]

    for g in range(2):
        ring_put(R3 + g, part(1, g, 1))
        ring_put(L3 + g, part(3, g, 0))

    for g in range(2):
        copies[R1 + g].wait_recv()
        ring_put(R2 + g, part(1, g, 0) + ring_get(R1 + g))
        ring_send(R2 + g, right)
        ring_send(R3 + g, right)
        copies[L1 + g].wait_recv()
        ring_put(L2 + g, part(3, g, 1) + ring_get(L1 + g))
        ring_send(L2 + g, left)
        ring_send(L3 + g, left)

    lane_live = lax.broadcasted_iota(I32, (128, half), 1) + b * rows
    csends = []
    for g in range(2):
        lo, hi = g * 128, (g + 1) * 128
        copies[L3 + g].wait_recv()
        copies[R2 + g].wait_recv()
        s = part(0, g, 0) + ring_get(L3 + g) + ring_get(R2 + g)
        sfin[lo:hi, 0:half] = jnp.where(lane_live < length, s, 0.0)
        copies[R3 + g].wait_recv()
        copies[L2 + g].wait_recv()
        s = part(0, g, 1) + ring_get(R3 + g) + ring_get(L2 + g)
        sfin[lo:hi, half:rows] = jnp.where(lane_live + half < length, s, 0.0)
        for k in range(8):
            zk = lax.dot_general(
                sfin[0:hi, k * 128 : (k + 1) * 128], mt[0:hi, lo:hi], (((0,), (0,)), ((), ())),
                precision=HI, preferred_element_type=F32,
            )
            q, e = encode_rows(zk)
            cq[g, k, 0:64, :] = q
            cq[g, k, 64:72, :] = e
        for m in range(16):
            cslot[g, m] = cq[g, source[m]]
        for i, o in enumerate(offs):
            cp = pltpu.make_async_remote_copy(
                src_ref=cslot.at[g, front_at(*o)], dst_ref=crecv.at[g, f],
                send_sem=c_send.at[g, i], recv_sem=c_recv.at[g, i],
                device_id={"front": front_at(*o)}, device_id_type=MESH,
            )
            cp.start()
            csends.append(cp)
        crecv[g, f] = cslot[g, f]

    weights = [[jnp.where(assign_ref[ch, 0] == p, 1.0, 0.0).astype(F32) for p in range(4)] for ch in range(16)]
    for cp in rsends:
        cp.wait_recv()

    @pl.loop(0, 4)
    def _(t):
        at = pl.ds(pl.multiple_of(t * 32, 32), 32)
        acc = [[jnp.zeros((32, 128), F32) for _ in range(2)] for _ in range(4)]
        for ch in range(16):
            q = rrecv[ch, at, :]
            ex = rrecv[ch, 128:129, :]
            for h, take in enumerate((low16, high16)):
                v = take(q).astype(F32)
                u = unscale(take(ex))
                for p in range(4):
                    acc[p][h] = acc[p][h] + v * (u * weights[ch][p])
        for p in range(4):
            row_ref[p, at, 0:128] = acc[p][0]
            row_ref[p, at, 128:256] = acc[p][1]

    for g in range(2):
        for cp in csends[g * 15 : (g + 1) * 15]:
            cp.wait_recv()

        @pl.loop(0, 2)
        def _(t):
            at = pl.ds(pl.multiple_of(t * 32, 32), 32)
            acc = [[jnp.zeros((32, 128), F32) for _ in range(2)] for _ in range(4)]
            for ch in range(16):
                q = crecv[g, ch, at, :]
                u = unscale(crecv[g, ch, 64:65, :])
                for h, take in enumerate((low16, high16)):
                    v = take(q).astype(F32)
                    for p in range(4):
                        acc[p][h] = acc[p][h] + v * (u * weights[ch][p])
            for p in range(4):
                for h in range(2):
                    rows_at = pl.ds(pl.multiple_of(h * 64 + t * 32, 32), 32)
                    col_ref[p, rows_at, g * 128 : (g + 1) * 128] = acc[p][h]

    for cp in own_right + own_left + [fwd_right, fwd_left] + list(cross.values()) + list(copies.values()):
        cp.wait_send()
    for dx in range(4):
        partial_to_partner(dx).wait_send()
    for cp in rsends + csends:
        cp.wait_send()


def on_device(contribution, omega_cols, psi_cols, lengths, selectors, assign, pivot_block):
    any_ref = pl.BlockSpec(memory_space=pl.ANY)
    smem = pl.BlockSpec(memory_space=pltpu.SMEM)
    vmem = pl.BlockSpec(memory_space=pltpu.VMEM)
    dma = pltpu.SemaphoreType.DMA
    row, col = pl.pallas_call(
        kernel,
        out_shape=[jax.ShapeDtypeStruct((4, 128, 256), F32)] * 2,
        in_specs=[any_ref, any_ref, any_ref, smem, smem, smem, any_ref],
        out_specs=[vmem, vmem],
        scratch_shapes=[
            pltpu.VMEM((8, 1024, 1024), BF16),
            pltpu.VMEM((8, 1024, 256), BF16),
            pltpu.VMEM((2, 1024, 256), BF16),
            pltpu.VMEM((256, 1024), BF16),
            pltpu.VMEM((4, 256, 256), F32),
            pltpu.VMEM((256, 512), F32),
            pltpu.VMEM((256, 256), F32),
            pltpu.VMEM((4, 256, 1024), F32),
            pltpu.VMEM((4, 256, 1024), F32),
            pltpu.VMEM((4, 256, 1024), F32),
            pltpu.VMEM((1024, 256), F32),
            pltpu.VMEM((256, 1024), F32),
            pltpu.VMEM((12, 136, 256), I32),
            pltpu.VMEM((12, 136, 256), I32),
            pltpu.VMEM((9, 136, 128), I32),
            pltpu.VMEM((16, 136, 128), I32),
            pltpu.VMEM((16, 136, 128), I32),
            pltpu.VMEM((2, 9, 72, 128), I32),
            pltpu.VMEM((2, 16, 72, 128), I32),
            pltpu.VMEM((2, 16, 72, 128), I32),
            dma((8,)),
            dma((3,)),
            dma((14,)),
            dma((14,)),
            dma((4,)),
            dma((4,)),
            dma((12,)),
            dma((12,)),
            dma((15,)),
            dma((15,)),
            dma((2, 15)),
            dma((2, 15)),
        ],
        compiler_params=pltpu.CompilerParams(
            collective_id=0, has_side_effects=True, vmem_limit_bytes=60 * 2**20
        ),
        cost_estimate=pl.CostEstimate(flops=9_000_000_000, bytes_accessed=20_000_000, transcendentals=0),
    )(contribution, omega_cols, psi_cols, lengths, selectors, assign, pivot_block)
    return (jnp.transpose(row, (1, 0, 2))[None], jnp.transpose(col, (1, 0, 2))[None])


def solution(mesh):
    in_specs = (
        P("front", "blk", None),
        P("front", "blk", None),
        P("front", "blk", None),
        P("front"),
        P("front", "blk"),
        P(),
        P(),
    )
    out_specs = (P("blk", "front", None, None), P("blk", "front", None, None))
    return jax.shard_map(
        on_device, mesh=mesh, in_specs=in_specs, out_specs=out_specs, check_vma=False
    )
```

time: 363 us -> 76.1 us (0.21)
  other arithmetic: 224 us -> 0 us
  Pallas kernels: 0 us -> 68.8 us
  waiting for transfers between devices: 65.4 us -> 0 us
  matrix products: 29.1 us -> 0 us
  local copies, waits for them, and re-layouts: 27.8 us -> 5.68 us
  between operations: 15.3 us -> 1.29 us
    another operation x13 -> x0, other arithmetic: 214 us -> none  [the longest x9 134 us: on_device(): factor = jnp.linalg.cholesky(pivot_block)]
    pallas_call x0 -> x1, Pallas kernels: none -> 68.8 us  [on_device(): pl.pallas_call(kernel, out_shape=[jax.ShapeDtypeStruct((4, 128, 256), F32...]
    reduce_scatter x1 -> x0, waiting for transfers between devices: 43.2 us -> none  [on_device(): lax.psum_scatter(lax.dot_general(block_cols, psi_live, (((0,), (0,)), (()...]
    dot_general x2 -> x0, matrix products: 24.2 us -> none  [the longest x1 13.9 us: on_device(): lax.dot_general(block_cols, psi_live, (((0,), (0,)), ((), ())), preferred...]
    all_gather x1 -> x0, waiting for transfers between devices: 21.5 us -> none  [on_device(): shard_rows = lax.all_gather(omega_local, 'blk', axis=0, tiled=True)]
    another operation x12 -> x0, local copies, waits for them, and re-layouts: 9.73 us -> none
    select_n x3 -> x0, other arithmetic: 9.56 us -> none  [the longest x1 8.06 us: on_device(): jnp.where(parent_mask, slab_rows, jnp.zeros_like(slab_rows))]
    transpose x2 -> x0, local copies, waits for them, and re-layouts: 8.18 us -> none  [the longest x1 7.78 us: on_device(): slab_rows = jnp.transpose(extended, (1, 0, 2))[:, :, None, :]]
  transfers between devices with their start and end apart: 3 -> 0, of which waited for: 2 -> 0; matrix products, arithmetic and copies ran while one was open for 68% -> 0% of each run, Pallas kernels for 0% -> 0%
where the time goes in v1:
time: 76.1 us; the launch traced here: 75.8 us
  Pallas kernels  68.8 us (90%)
  local copies, waits for them, and re-layouts  5.68 us (7%)
  between operations  1.29 us (2%)
    pallas_call x1, Pallas kernels, on_device(): pl.pallas_call(kernel, out_shape=[jax.ShapeDtypeStruct((4, 128, 256), F32...  68.8 us
    unnamed x3, local copies, waits for them, and re-layouts  5.68 us

profile of v1, /device:TPU:1, one launch (start us, length us, event | category | flops | bytes accessed | tf_op | source)
XLA Modules:
  0.0 75.8 jit_solution(9499211041515881092)
XLA Ops:
  1.3 1.3 %copy.9.assign_ref = s32[16,1]{1,0:T(8,128)} copy(s32[16,1]{0,1:T(1,128)} %param.12) | data formatting | bytes 128 | tf_op args[5]
  2.6 68.8 %shard_map.86 = (f32[4,128,256]{2,1,0:T(8,128)}, f32[4,128,256]{2,1,0:T(8,128)}) custom-call(bf16[1,1024,8192]{2,1,0:T(8,128)(2,1)} %front_ref.1, bf16[1,1024,256]{2,1,0:T(8,128)(2,1)} %omega_ref.1, bf16[1,1024,256]{2,1,0:T(8,128)(2,1)} %psi_ref.1, s32[1]{0:T(128)S(6)} %copy.12.length_ref, s32[1,8]{1,0:T(1,128)} %chosen_ref.1, s32[16,1]{1,0:T(8,128)} %copy.9.assign_ref, ...), custom_call_target="tpu_custom_call" | custom-call | flops 8999999488 | bytes 20000000 | tf_op jit(solution)/shard_map/pallas_call | solution.py:420
  71.4 2.2 %copy.10 = f32[1,128,4,256]{3,2,1,0:T(4,128)} copy(f32[1,128,4,256]{3,1,2,0:T(8,128)} %bitcast.7) | data formatting | bytes 1048576
  73.6 2.2 %copy.11 = f32[1,128,4,256]{3,2,1,0:T(4,128)} copy(f32[1,128,4,256]{3,1,2,0:T(8,128)} %bitcast.6) | data formatting | bytes 1048576

commit v2 on v1

v2 whole, which is shorter than its diff:
```python
import functools

import jax
import jax.numpy as jnp
from jax import lax
from jax.experimental import pallas as pl
from jax.experimental.pallas import tpu as pltpu
from jax.sharding import PartitionSpec as P

MESH = pl.DeviceIdType.MESH
HI = lax.Precision.HIGHEST
F32 = jnp.float32
I32 = jnp.int32
BF16 = jnp.bfloat16
NB = 64
TOP = 32766.0


def join16(t, axis):
    half = t.shape[axis] // 2
    low = lax.slice_in_dim(t, 0, half, axis=axis)
    high = lax.slice_in_dim(t, half, 2 * half, axis=axis)
    return (high << 16) | (low & 0xFFFF)


def scale_of(v):
    m = jnp.max(jnp.abs(v), axis=0, keepdims=True)
    e = jnp.floor(jnp.log2(jnp.maximum(m, 2.0**-100))) + 1.0
    return e, jnp.exp2(-e) * TOP


def encode_lanes(v):
    e, factor = scale_of(v)
    q = jnp.round(v * factor).astype(I32)
    ex = join16(e.astype(I32), 1)
    return join16(q, 1), ex


def encode_rows(v):
    e, factor = scale_of(v)
    q = jnp.round(v * factor).astype(I32)
    return join16(q, 0), e.astype(I32)


def low16(t):
    return (t << 16) >> 16


def high16(t):
    return t >> 16


def unscale(e):
    return jnp.exp2(e.astype(F32)) * (1.0 / TOP)


def decode_lanes(ref, rows):
    ex = ref[rows : rows + 1, :]
    q = ref[0:rows, :]
    low = low16(q).astype(F32) * unscale(low16(ex))
    high = high16(q).astype(F32) * unscale(high16(ex))
    return jnp.concatenate([low, high], axis=1)


def split(t):
    high = t.astype(BF16)
    return high, (t - high.astype(F32)).astype(BF16)


def dot_split(s, m_high, m_low):
    high, low = split(s)
    dot = lambda p, q: jnp.dot(p, q, preferred_element_type=F32)
    return dot(high, m_high) + (dot(low, m_high) + dot(high, m_low))


def factor_block(w, blk):
    n = w.shape[0]
    o = blk * NB
    r8 = lax.broadcasted_iota(I32, (8, 128), 0)
    wb = w[o : o + NB, :]
    wide = wb.shape[1] // 128
    tile = lambda f: jnp.concatenate([f] * wide, axis=1)
    strips = [wb[8 * s : 8 * s + 8, :] for s in range(NB // 8)]
    for s in range(NB // 8):
        so = o + 8 * s
        left = NB // 8 - s
        cols = [
            [jnp.broadcast_to(strips[t][:, so + k : so + k + 1], (8, 128)) for k in range(8)]
            for t in range(s, NB // 8)
        ]
        st = strips[s]
        scale = jnp.zeros((8, 128), F32)
        fs = [[None] * 8 for _ in range(left)]
        for k in range(8):
            pivot = jnp.broadcast_to(cols[0][k][k : k + 1, :], (8, 128))
            inverse = 1.0 / pivot
            scale = jnp.where(r8 == k, lax.rsqrt(pivot), scale)
            for t in range(left):
                f = cols[t][k] * inverse
                fs[t][k] = jnp.where(r8 > k, f, 0.0) if t == 0 else f
            for j in range(k + 1, 8):
                u = jnp.broadcast_to(cols[0][j][k : k + 1, :], (8, 128))
                for t in range(left):
                    cols[t][j] = cols[t][j] - fs[t][k] * u
        for k in range(8):
            st = st - tile(fs[0][k]) * jnp.broadcast_to(st[k : k + 1, :], st.shape)
        for t in range(1, left):
            acc = strips[s + t]
            for k in range(8):
                acc = acc - tile(fs[t][k]) * jnp.broadcast_to(st[k : k + 1, :], st.shape)
            strips[s + t] = acc
        strips[s] = st
        w[so : so + 8, :] = st * tile(scale)
    if o + NB < n:
        y = w[o : o + NB, :]
        later = y[:, o + NB : n]
        w[o + NB : n, :] = w[o + NB : n, :] - lax.dot_general(
            later, y, (((0,), (0,)), ((), ())), precision=HI, preferred_element_type=F32
        )


def kernel(
    front_ref, omega_ref, psi_ref, length_ref, chosen_ref, assign_ref, pivot_ref,
    row_ref, col_ref,
    cbuf, ombuf, raw, psit, pivots, w, mt, psend, pown, precv, racc, sfin,
    xsend, xrecv, quant, slots, arrived,
    csem, insem, om_send, om_recv, p_send, p_recv, x_send, x_recv, s_send, s_recv,
):
    f = lax.axis_index("front")
    b = lax.axis_index("blk")
    X = b // 2
    c = lax.rem(b, 2)
    rows = 1024
    half = rows // 2
    blk_at = lambda dx, core: lax.rem(X + dx, 4) * 2 + core
    right = {"blk": blk_at(1, c)}
    left = {"blk": blk_at(3, c)}
    partner = {"blk": blk_at(0, 1 - c)}
    z, y = f // 4, lax.rem(f, 4)
    offs = [(dz, dy) for dz in range(4) for dy in range(4)][1:]
    front_at = lambda dz, dy: lax.rem(z + dz, 4) * 4 + lax.rem(y + dy, 4)

    barrier = pltpu.get_barrier_semaphore()
    peers = [right, left, partner] + [{"front": front_at(*o)} for o in offs]
    for peer in peers:
        pl.semaphore_signal(barrier, inc=1, device_id=peer, device_id_type=MESH)

    omega_in = pltpu.make_async_copy(omega_ref.at[0], raw.at[0], insem.at[0])
    psi_in = pltpu.make_async_copy(psi_ref.at[0], raw.at[1], insem.at[1])
    pivot_in = pltpu.make_async_copy(pivot_ref, pivots, insem.at[2])
    omega_in.start()
    psi_in.start()

    def chunk_in(dx, core):
        j = blk_at(dx, core)
        return pltpu.make_async_copy(
            front_ref.at[0, :, pl.ds(pl.multiple_of(j * rows, rows), rows)], cbuf.at[j], csem.at[j]
        )

    length = length_ref[0]
    live = lax.broadcasted_iota(I32, (rows, 128), 0) + b * rows < length

    omega_in.wait()
    for k in range(4):
        chunk_in((k + 2) % 4, 1 - c).start()
        chunk_in((k + 2) % 4, c).start()
    pivot_in.start()
    for g in range(2):
        ombuf[g, b] = jnp.where(live, raw[0, :, g * 128 : (g + 1) * 128].astype(F32), 0.0).astype(BF16)
    pl.semaphore_wait(barrier, len(peers))

    sent = []

    def piece(g, blk, h, sem, to):
        ref = ombuf.at[g, blk, pl.ds(h * half, half)]
        cp = pltpu.make_async_remote_copy(
            src_ref=ref, dst_ref=ref, send_sem=om_send.at[g, sem], recv_sem=om_recv.at[g, sem],
            device_id=to, device_id_type=MESH,
        )
        cp.start()
        sent.append(cp)
        return cp

    cross = {}

    def cross_send(g, dx, h):
        cross[g, dx, h] = piece(g, blk_at(dx, c), h, 6 + dx * 2 + h, partner)

    own = {}
    for h in range(2):
        own[0, 0, h] = piece(0, b, h, h, right)
        own[0, 1, 1 - h] = piece(0, b, 1 - h, 3 - h, left)
    for g in range(2):
        for h in range(2):
            cross_send(g, 0, h)

    psi_in.wait()
    live_all = lax.broadcasted_iota(I32, (rows, 256), 0) + b * rows < length
    psit[...] = jnp.where(live_all, raw[1].astype(F32), 0.0).T.astype(BF16)

    def partial_to_partner(dx):
        return pltpu.make_async_remote_copy(
            src_ref=psend.at[dx], dst_ref=precv.at[dx], send_sem=p_send.at[dx], recv_sem=p_recv.at[dx],
            device_id=partner, device_id_type=MESH,
        )

    @pl.loop(0, 4)
    def _(k):
        dx = lax.rem(k + 2, 4)
        chunk_in(dx, 1 - c).wait()
        psend[dx] = jnp.dot(psit[...], cbuf[blk_at(dx, 1 - c)], preferred_element_type=F32)
        partial_to_partner(dx).start()
        chunk_in(dx, c).wait()
        pown[dx] = jnp.dot(psit[...], cbuf[blk_at(dx, c)], preferred_element_type=F32)

    def row_add(g, dx, core, h, first=False):
        blk = blk_at(dx, core)
        t = jnp.dot(
            cbuf[blk, :, h * half : (h + 1) * half], ombuf[g, blk, h * half : (h + 1) * half, :],
            preferred_element_type=F32,
        )
        racc[g] = t if first else racc[g] + t

    def row_adds(g, pieces, first=False):
        @pl.loop(0, 2)
        def _(t):
            at = pl.ds(pl.multiple_of(t * 512, 512), 512)
            acc = None if first else racc[g, at, :]
            for dx, core, h in pieces:
                blk = blk_at(dx, core)
                v = jnp.dot(
                    cbuf[blk, at, h * half : (h + 1) * half], ombuf[g, blk, h * half : (h + 1) * half, :],
                    preferred_element_type=F32,
                )
                acc = v if acc is None else acc + v
            racc[g, at, :] = acc

    both = lambda pieces: [(dx, core, h) for dx, h in pieces for core in (c, 1 - c)]

    def row_add_own(g):
        for h in range(2):
            row_add(g, 0, c, h, h == 0)
            row_add(g, 0, 1 - c, h)

    def row_add_near(g, pieces):
        for dx, h in pieces:
            row_add(g, dx, c, h)
            row_add(g, dx, 1 - c, h)

    near_first, near_second = ((3, 0), (1, 1)), ((3, 1), (1, 0))

    own[1, 0, 0] = piece(1, b, 0, 0, right)
    own[1, 1, 1] = piece(1, b, 1, 3, left)
    passed = {}

    def pass_on(g):
        own[g, 0, 0].wait_recv()
        passed[g, 0] = piece(g, blk_at(3, c), 0, 4, right)
        cross_send(g, 3, 0)
        own[g, 1, 1].wait_recv()
        passed[g, 1] = piece(g, blk_at(1, c), 1, 5, left)
        cross_send(g, 1, 1)

    def cross_second(g):
        own[g, 0, 1].wait_recv()
        cross_send(g, 3, 1)
        own[g, 1, 0].wait_recv()
        cross_send(g, 1, 0)

    def cross_third(g):
        for h in range(2):
            passed[g, h].wait_recv()
            cross_send(g, 2, h)

    def wait_cross(g, pieces):
        for dx, h in pieces:
            cross[g, dx, h].wait_recv()

    pass_on(0)

    pivot_in.wait()
    parent = assign_ref[f]
    w[:, 0:256] = pivots[parent]
    eye = lax.broadcasted_iota(I32, (256, 256), 0) == lax.broadcasted_iota(I32, (256, 256), 1)
    w[:, 256:512] = jnp.where(eye, 1.0, 0.0)
    wait_cross(0, ((0, 0), (0, 1)))
    row_add_own(0)
    factor_block(w, 0)
    own[1, 0, 1] = piece(1, b, 1, 1, right)
    own[1, 1, 0] = piece(1, b, 0, 2, left)
    cross_second(0)
    wait_cross(0, near_first)
    row_add_near(0, near_first)
    factor_block(w, 1)

    def keep_inverse(g):
        m_high, m_low = split(w[g * 128 : (g + 1) * 128, 256:512].T)
        mt[0, :, g * 128 : (g + 1) * 128] = m_high
        mt[1, :, g * 128 : (g + 1) * 128] = m_low

    keep_inverse(0)

    for dx in (2, 1, 3, 0):
        partial_to_partner(dx).wait_recv()
        pown[dx] = pown[dx] + precv[dx]

    def ring_put(sem, v):
        q, e = encode_lanes(v)
        xsend[sem, 0:128, :] = q
        xsend[sem, 128:129, :] = e

    ring_get = lambda sem: decode_lanes(xrecv.at[sem], 128)
    copies = {}

    def ring_send(sem, to):
        copies[sem] = pltpu.make_async_remote_copy(
            src_ref=xsend.at[sem], dst_ref=xrecv.at[sem], send_sem=x_send.at[sem], recv_sem=x_recv.at[sem],
            device_id=to, device_id_type=MESH,
        )
        copies[sem].start()
        sent.append(copies[sem])

    part = lambda dx, g, h: pown[dx, g * 128 : (g + 1) * 128, h * half : (h + 1) * half]
    R1, R2, R3, L1, L2, L3 = 0, 2, 4, 6, 8, 10
    for g in range(2):
        ring_put(R1 + g, part(2, g, 0))
        ring_put(L1 + g, part(2, g, 1))
    for g in range(2):
        ring_put(R3 + g, part(1, g, 1))
        ring_put(L3 + g, part(3, g, 0))
    wait_cross(1, ((0, 0), (0, 1)))
    row_adds(1, both(((0, 0), (0, 1))), True)

    cross_third(0)
    pass_on(1)
    wait_cross(0, near_second)
    row_adds(0, both(near_second) + [(2, c, 0), (2, c, 1)])
    wait_cross(0, ((2, 0), (2, 1)))
    row_adds(0, [(2, 1 - c, 0), (2, 1 - c, 1)])

    for mat in range(2):
        for g in range(2):
            quant[mat, g, 8] = jnp.zeros(quant.shape[3:], I32)
    source = []
    for m in range(16):
        at = jnp.int32(8)
        for k in range(8):
            at = jnp.where(chosen_ref[0, k] == m, jnp.int32(k), at)
        source.append(at)
    placed = {}

    def place(mat, g):
        for m in range(16):
            slots[mat, g, m] = quant[mat, g, source[m]]
        placed[mat, g] = []
        for i, o in enumerate(offs):
            cp = pltpu.make_async_remote_copy(
                src_ref=slots.at[mat, g, front_at(*o)], dst_ref=arrived.at[mat, g, f],
                send_sem=s_send.at[mat, g, i], recv_sem=s_recv.at[mat, g, i],
                device_id={"front": front_at(*o)}, device_id_type=MESH,
            )
            cp.start()
            sent.append(cp)
            placed[mat, g].append(cp)
        arrived[mat, g, f] = slots[mat, g, f]

    def keep_quant(mat, g, k, zk):
        q, e = encode_rows(zk)
        quant[mat, g, k, 0:64, :] = q
        quant[mat, g, k, 64:65, :] = e

    sub_live = lax.broadcasted_iota(I32, (128, 128), 0) + b * rows

    def solve_rows(g):
        hi = (g + 1) * 128
        for k in range(8):
            parts = [racc[t, k * 128 : (k + 1) * 128, :] for t in range(g + 1)]
            s = jnp.concatenate([jnp.where(sub_live + k * 128 < length, t, 0.0) for t in parts], axis=1)
            keep_quant(0, g, k, dot_split(s, mt[0, 0:hi, hi - 128 : hi], mt[1, 0:hi, hi - 128 : hi]))
        place(0, g)

    solve_rows(0)

    ring_send(R1, right)
    ring_send(L1, left)
    cross_third(1)
    cross_second(1)
    wait_cross(1, near_first)
    wait_cross(1, near_second)
    row_add_near(1, near_first)
    row_add_near(1, near_second)
    factor_block(w, 2)
    ring_send(R1 + 1, right)
    ring_send(L1 + 1, left)
    wait_cross(1, ((2, 0), (2, 1)))
    for h in range(2):
        row_add(1, 2, c, h)
        row_add(1, 2, 1 - c, h)
    factor_block(w, 3)
    keep_inverse(1)

    def ring_middle(g):
        copies[R1 + g].wait_recv()
        ring_put(R2 + g, part(1, g, 0) + ring_get(R1 + g))
        ring_send(R2 + g, right)
        ring_send(R3 + g, right)
        copies[L1 + g].wait_recv()
        ring_put(L2 + g, part(3, g, 1) + ring_get(L1 + g))
        ring_send(L2 + g, left)
        ring_send(L3 + g, left)

    ring_middle(0)
    solve_rows(1)
    ring_middle(1)

    lane_live = lax.broadcasted_iota(I32, (128, half), 1) + b * rows

    def finish_columns(g):
        lo, hi = g * 128, (g + 1) * 128
        copies[L3 + g].wait_recv()
        copies[R2 + g].wait_recv()
        s = part(0, g, 0) + ring_get(L3 + g) + ring_get(R2 + g)
        sfin[lo:hi, 0:half] = jnp.where(lane_live < length, s, 0.0)
        copies[R3 + g].wait_recv()
        copies[L2 + g].wait_recv()
        s = part(0, g, 1) + ring_get(R3 + g) + ring_get(L2 + g)
        sfin[lo:hi, half:rows] = jnp.where(lane_live + half < length, s, 0.0)
        for k in range(8):
            s = sfin[0:hi, k * 128 : (k + 1) * 128].T
            keep_quant(1, g, k, dot_split(s, mt[0, 0:hi, lo:hi], mt[1, 0:hi, lo:hi]))
        place(1, g)

    weights = [[jnp.where(assign_ref[ch] == p, 1.0, 0.0).astype(F32) for p in range(4)] for ch in range(16)]

    def gather(mat, g):
        for cp in placed[mat, g]:
            cp.wait_recv()
        out = (row_ref, col_ref)[mat]

        @pl.loop(0, 2)
        def _(t):
            at = pl.ds(pl.multiple_of(t * 32, 32), 32)
            acc = [[jnp.zeros((32, 128), F32) for _ in range(2)] for _ in range(4)]
            for ch in range(16):
                q = arrived[mat, g, ch, at, :]
                u = unscale(arrived[mat, g, ch, 64:65, :])
                for h, take in enumerate((low16, high16)):
                    v = take(q).astype(F32)
                    for p in range(4):
                        acc[p][h] = acc[p][h] + v * (u * weights[ch][p])
            for p in range(4):
                for h in range(2):
                    out[pl.ds(h * 512 + t * 256 + g * 4 + p, 32, stride=8), :] = acc[p][h]

    gather(0, 0)
    finish_columns(0)
    gather(0, 1)
    finish_columns(1)
    gather(1, 0)
    gather(1, 1)

    for cp in sent:
        cp.wait_send()
    for dx in range(4):
        partial_to_partner(dx).wait_send()


def panel_of(t):
    return jnp.transpose(t.reshape(1, 128, 2, 4, 128), (0, 1, 3, 2, 4)).reshape(1, 128, 4, 256)


def on_device(contribution, omega_cols, psi_cols, lengths, selectors, assign, pivot_block):
    any_ref = pl.BlockSpec(memory_space=pl.ANY)
    smem = pl.BlockSpec(memory_space=pltpu.SMEM)
    vmem = pl.BlockSpec(memory_space=pltpu.VMEM)
    dma = pltpu.SemaphoreType.DMA
    row, col = pl.pallas_call(
        kernel,
        out_shape=[jax.ShapeDtypeStruct((1024, 128), F32)] * 2,
        in_specs=[any_ref, any_ref, any_ref, smem, smem, smem, any_ref],
        out_specs=[vmem, vmem],
        scratch_shapes=[
            pltpu.VMEM((8, 1024, 1024), BF16),
            pltpu.VMEM((2, 8, 1024, 128), BF16),
            pltpu.VMEM((2, 1024, 256), BF16),
            pltpu.VMEM((256, 1024), BF16),
            pltpu.VMEM((4, 256, 256), F32),
            pltpu.VMEM((256, 512), F32),
            pltpu.VMEM((2, 256, 256), BF16),
            pltpu.VMEM((4, 256, 1024), F32),
            pltpu.VMEM((4, 256, 1024), F32),
            pltpu.VMEM((4, 256, 1024), F32),
            pltpu.VMEM((2, 1024, 128), F32),
            pltpu.VMEM((256, 1024), F32),
            pltpu.VMEM((12, 129, 256), I32),
            pltpu.VMEM((12, 129, 256), I32),
            pltpu.VMEM((2, 2, 9, 65, 128), I32),
            pltpu.VMEM((2, 2, 16, 65, 128), I32),
            pltpu.VMEM((2, 2, 16, 65, 128), I32),
            dma((8,)),
            dma((3,)),
            dma((2, 14)),
            dma((2, 14)),
            dma((4,)),
            dma((4,)),
            dma((12,)),
            dma((12,)),
            dma((2, 2, 15)),
            dma((2, 2, 15)),
        ],
        compiler_params=pltpu.CompilerParams(
            collective_id=0, has_side_effects=True, vmem_limit_bytes=60 * 2**20
        ),
        cost_estimate=pl.CostEstimate(flops=9_000_000_000, bytes_accessed=20_000_000, transcendentals=0),
    )(contribution, omega_cols, psi_cols, lengths, selectors, assign.reshape(-1), pivot_block)
    row, col = (jnp.where(lengths[0] > 0, t, 0.0) for t in (row, col))
    return (panel_of(row), panel_of(col))


def solution(mesh):
    in_specs = (
        P("front", "blk", None),
        P("front", "blk", None),
        P("front", "blk", None),
        P("front"),
        P("front", "blk"),
        P(),
        P(),
    )
    out_specs = (P("blk", "front", None, None), P("blk", "front", None, None))
    return jax.shard_map(
        on_device, mesh=mesh, in_specs=in_specs, out_specs=out_specs, check_vma=False
    )
```

time: 76.1 us -> 67.2 us (0.88)
  local copies, waits for them, and re-layouts: 5.68 us -> 0 us
  Pallas kernels: 68.8 us -> 63.5 us
  other arithmetic: 0 us -> 2.24 us
    unnamed x3 -> x0, local copies, waits for them, and re-layouts: 5.68 us -> none
    pallas_call x1, Pallas kernels: 68.8 us -> 63.5 us  [on_device(): pl.pallas_call(kernel, out_shape=[jax.ShapeDtypeStruct((1024, 128), F32)]...]
    select_n x0 -> x1, other arithmetic: none -> 2.24 us  [on_device(): row, col = (jnp.where(lengths[0] > 0, t, 0.0) for t in (row, col))]
where the time goes in v2:
time: 67.2 us; the launch traced here: 67 us
  Pallas kernels  63.5 us (94%)
  other arithmetic  2.24 us (3%)
  between operations  1.29 us (2%)
    pallas_call x1, Pallas kernels, on_device(): pl.pallas_call(kernel, out_shape=[jax.ShapeDtypeStruct((1024, 128), F32)]...  63.5 us
    select_n x1, other arithmetic, on_device(): row, col = (jnp.where(lengths[0] > 0, t, 0.0) for t in (row, col))  2.24 us

profile of v2, /device:TPU:1, one launch (start us, length us, event | category | flops | bytes accessed | tf_op | source)
XLA Modules:
  0.0 67.0 jit_solution(12615174520731619744)
XLA Ops:
  1.3 63.5 %shard_map.86 = (f32[1024,128]{1,0:T(8,128)}, f32[1024,128]{1,0:T(8,128)}) custom-call(bf16[1,1024,8192]{2,1,0:T(8,128)(2,1)} %front_ref.1, bf16[1,1024,256]{2,1,0:T(8,128)(2,1)} %omega_ref.1, bf16[1,1024,256]{2,1,0:T(8,128)(2,1)} %psi_ref.1, s32[1]{0:T(128)S(6)} %copy.11.length_ref, s32[1,8]{1,0:T(1,128)} %chosen_ref.1, s32[16]{0:T(128)} %bitcast.14, ...), custom_call_target="tpu_custom_call" | custom-call | flops 8999999488 | bytes 20000000 | tf_op jit(solution)/shard_map/pallas_call | solution.py:477
  64.8 2.2 %broadcast_select_fusion = (f32[1024,128]{1,0:T(8,128)}, f32[1024,128]{1,0:T(8,128)}) fusion(f32[1024,128]{1,0:T(8,128)} %get-tuple-element.5, pred[]{:T(512)} %bitcast, f32[1024,128]{1,0:T(8,128)} %get-tuple-element.4), kind=kLoop, calls=%fused_computation | loop fusion | flops 262144 | bytes 2097153 | tf_op jit(solution)/shard_map/jit(_where)/select_n | solution.py:516

commit v3 on v2

--- a/solution.py
+++ b/solution.py
@@ -120,9 +120,9 @@
 
 
 def kernel(
-    front_ref, omega_ref, psi_ref, length_ref, chosen_ref, assign_ref, pivot_ref,
-    row_ref, col_ref,
-    cbuf, ombuf, raw, psit, pivots, w, mt, psend, pown, precv, racc, sfin,
+    front_ref, omega_ref, psi_ref, length_in, chosen_in, assign_in, pivot_ref,
+    row_out, col_out,
+    length_ref, chosen_ref, assign_ref, row_ref, col_ref, cbuf, ombuf, raw, psit, pivots, w, mt, psend, pown, precv, racc, sfin,
     xsend, xrecv, quant, slots, arrived,
     csem, insem, om_send, om_recv, p_send, p_recv, x_send, x_recv, s_send, s_recv,
 ):
@@ -137,7 +137,8 @@
     left = {"blk": blk_at(3, c)}
     partner = {"blk": blk_at(0, 1 - c)}
     z, y = f // 4, lax.rem(f, 4)
-    offs = [(dz, dy) for dz in range(4) for dy in range(4)][1:]
+    hops = lambda o: min(o[0], 4 - o[0]) + min(o[1], 4 - o[1])
+    offs = sorted([(dz, dy) for dz in range(4) for dy in range(4)][1:], key=lambda o: -hops(o))
     front_at = lambda dz, dy: lax.rem(z + dz, 4) * 4 + lax.rem(y + dy, 4)
 
     barrier = pltpu.get_barrier_semaphore()
@@ -149,6 +150,14 @@
     psi_in = pltpu.make_async_copy(psi_ref.at[0], raw.at[1], insem.at[1])
     pivot_in = pltpu.make_async_copy(pivot_ref, pivots, insem.at[2])
     omega_in.start()
+    scalars_in = [
+        pltpu.make_async_copy(source, to, insem.at[5 + i])
+        for i, (source, to) in enumerate(
+            ((length_in, length_ref), (chosen_in, chosen_ref), (assign_in, assign_ref))
+        )
+    ]
+    for cp in scalars_in:
+        cp.start()
     psi_in.start()
 
     def chunk_in(dx, core):
@@ -157,6 +166,8 @@
             front_ref.at[0, :, pl.ds(pl.multiple_of(j * rows, rows), rows)], cbuf.at[j], csem.at[j]
         )
 
+    for cp in scalars_in:
+        cp.wait()
     length = length_ref[0]
     live = lax.broadcasted_iota(I32, (rows, 128), 0) + b * rows < length
 
@@ -186,13 +197,24 @@
     def cross_send(g, dx, h):
         cross[g, dx, h] = piece(g, blk_at(dx, c), h, 6 + dx * 2 + h, partner)
 
-    own = {}
-    for h in range(2):
-        own[0, 0, h] = piece(0, b, h, h, right)
-        own[0, 1, 1 - h] = piece(0, b, 1 - h, 3 - h, left)
+    own, passed = {}, {}
+    own[0, 0, 0] = piece(0, b, 0, 0, right)
+    own[0, 1, 1] = piece(0, b, 1, 3, left)
     for g in range(2):
         for h in range(2):
             cross_send(g, 0, h)
+
+    def own_second(g):
+        own[g, 0, 1] = piece(g, b, 1, 1, right)
+        own[g, 1, 0] = piece(g, b, 0, 2, left)
+
+    def pass_on(g):
+        own[g, 0, 0].wait_recv()
+        passed[g, 0] = piece(g, blk_at(3, c), 0, 4, right)
+        cross_send(g, 3, 0)
+        own[g, 1, 1].wait_recv()
+        passed[g, 1] = piece(g, blk_at(1, c), 1, 5, left)
+        cross_send(g, 1, 1)
 
     psi_in.wait()
     live_all = lax.broadcasted_iota(I32, (rows, 256), 0) + b * rows < length
@@ -204,14 +226,20 @@
             device_id=partner, device_id_type=MESH,
         )
 
-    @pl.loop(0, 4)
-    def _(k):
-        dx = lax.rem(k + 2, 4)
+    def column_partials(k):
+        dx = (k + 2) % 4
         chunk_in(dx, 1 - c).wait()
         psend[dx] = jnp.dot(psit[...], cbuf[blk_at(dx, 1 - c)], preferred_element_type=F32)
         partial_to_partner(dx).start()
         chunk_in(dx, c).wait()
         pown[dx] = jnp.dot(psit[...], cbuf[blk_at(dx, c)], preferred_element_type=F32)
+
+    column_partials(0)
+    column_partials(1)
+    own_second(0)
+    column_partials(2)
+    pass_on(0)
+    column_partials(3)
 
     def row_add(g, dx, core, h, first=False):
         blk = blk_at(dx, core)
@@ -249,18 +277,6 @@
 
     near_first, near_second = ((3, 0), (1, 1)), ((3, 1), (1, 0))
 
-    own[1, 0, 0] = piece(1, b, 0, 0, right)
-    own[1, 1, 1] = piece(1, b, 1, 3, left)
-    passed = {}
-
-    def pass_on(g):
-        own[g, 0, 0].wait_recv()
-        passed[g, 0] = piece(g, blk_at(3, c), 0, 4, right)
-        cross_send(g, 3, 0)
-        own[g, 1, 1].wait_recv()
-        passed[g, 1] = piece(g, blk_at(1, c), 1, 5, left)
-        cross_send(g, 1, 1)
-
     def cross_second(g):
         own[g, 0, 1].wait_recv()
         cross_send(g, 3, 1)
@@ -275,8 +291,6 @@
     def wait_cross(g, pieces):
         for dx, h in pieces:
             cross[g, dx, h].wait_recv()
-
-    pass_on(0)
 
     pivot_in.wait()
     parent = assign_ref[f]
@@ -286,8 +300,8 @@
     wait_cross(0, ((0, 0), (0, 1)))
     row_add_own(0)
     factor_block(w, 0)
-    own[1, 0, 1] = piece(1, b, 1, 1, right)
-    own[1, 1, 0] = piece(1, b, 0, 2, left)
+    own[1, 0, 0] = piece(1, b, 0, 0, right)
+    own[1, 1, 1] = piece(1, b, 1, 3, left)
     cross_second(0)
     wait_cross(0, near_first)
     row_add_near(0, near_first)
@@ -300,6 +314,8 @@
 
     keep_inverse(0)
 
+    cross_third(0)
+    own_second(1)
     for dx in (2, 1, 3, 0):
         partial_to_partner(dx).wait_recv()
         pown[dx] = pown[dx] + precv[dx]
@@ -328,13 +344,9 @@
     for g in range(2):
         ring_put(R3 + g, part(1, g, 1))
         ring_put(L3 + g, part(3, g, 0))
-    wait_cross(1, ((0, 0), (0, 1)))
-    row_adds(1, both(((0, 0), (0, 1))), True)
-
-    cross_third(0)
-    pass_on(1)
     wait_cross(0, near_second)
     row_adds(0, both(near_second) + [(2, c, 0), (2, c, 1)])
+    pass_on(1)
     wait_cross(0, ((2, 0), (2, 1)))
     row_adds(0, [(2, 1 - c, 0), (2, 1 - c, 1)])
 
@@ -380,22 +392,16 @@
         place(0, g)
 
     solve_rows(0)
-
     ring_send(R1, right)
     ring_send(L1, left)
-    cross_third(1)
-    cross_second(1)
-    wait_cross(1, near_first)
-    wait_cross(1, near_second)
-    row_add_near(1, near_first)
-    row_add_near(1, near_second)
+    wait_cross(1, ((0, 0), (0, 1)))
+    row_add_own(1)
     factor_block(w, 2)
     ring_send(R1 + 1, right)
     ring_send(L1 + 1, left)
-    wait_cross(1, ((2, 0), (2, 1)))
-    for h in range(2):
-        row_add(1, 2, c, h)
-        row_add(1, 2, 1 - c, h)
+    cross_second(1)
+    wait_cross(1, near_first)
+    row_add_near(1, near_first)
     factor_block(w, 3)
     keep_inverse(1)
 
@@ -410,6 +416,11 @@
         ring_send(L3 + g, left)
 
     ring_middle(0)
+    cross_third(1)
+    wait_cross(1, near_second)
+    row_adds(1, both(near_second) + [(2, c, 0), (2, c, 1)])
+    wait_cross(1, ((2, 0), (2, 1)))
+    row_adds(1, [(2, 1 - c, 0), (2, 1 - c, 1)])
     solve_rows(1)
     ring_middle(1)
 
@@ -455,14 +466,20 @@
     gather(0, 0)
     finish_columns(0)
     gather(0, 1)
+    row_done = pltpu.make_async_copy(row_ref, row_out, insem.at[3])
+    row_done.start()
     finish_columns(1)
     gather(1, 0)
     gather(1, 1)
+    col_done = pltpu.make_async_copy(col_ref, col_out, insem.at[4])
+    col_done.start()
 
     for cp in sent:
         cp.wait_send()
     for dx in range(4):
         partial_to_partner(dx).wait_send()
+    row_done.wait()
+    col_done.wait()
 
 
 def panel_of(t):
@@ -471,15 +488,19 @@
 
 def on_device(contribution, omega_cols, psi_cols, lengths, selectors, assign, pivot_block):
     any_ref = pl.BlockSpec(memory_space=pl.ANY)
-    smem = pl.BlockSpec(memory_space=pltpu.SMEM)
-    vmem = pl.BlockSpec(memory_space=pltpu.VMEM)
+    hbm = pl.BlockSpec(memory_space=pl.ANY)
     dma = pltpu.SemaphoreType.DMA
     row, col = pl.pallas_call(
         kernel,
         out_shape=[jax.ShapeDtypeStruct((1024, 128), F32)] * 2,
-        in_specs=[any_ref, any_ref, any_ref, smem, smem, smem, any_ref],
-        out_specs=[vmem, vmem],
+        in_specs=[hbm] * 7,
+        out_specs=[any_ref, any_ref],
         scratch_shapes=[
+            pltpu.SMEM((1,), I32),
+            pltpu.SMEM((1, 8), I32),
+            pltpu.SMEM((16,), I32),
+            pltpu.VMEM((1024, 128), F32),
+            pltpu.VMEM((1024, 128), F32),
             pltpu.VMEM((8, 1024, 1024), BF16),
             pltpu.VMEM((2, 8, 1024, 128), BF16),
             pltpu.VMEM((2, 1024, 256), BF16),
@@ -498,7 +519,7 @@
             pltpu.VMEM((2, 2, 16, 65, 128), I32),
             pltpu.VMEM((2, 2, 16, 65, 128), I32),
             dma((8,)),
-            dma((3,)),
+            dma((8,)),
             dma((2, 14)),
             dma((2, 14)),
             dma((4,)),

time: 67.2 us -> 60.7 us (0.903)
  Pallas kernels: 63.5 us -> 56.5 us
    pallas_call x1, Pallas kernels: 63.5 us -> 56.5 us  [on_device(): pl.pallas_call(kernel, out_shape=[jax.ShapeDtypeStruct((1024, 128), F32)]...]
where the time goes in v3:
time: 60.7 us; the launch traced here: 60 us
  Pallas kernels  56.5 us (93%)
  other arithmetic  2.24 us (4%)
  between operations  1.29 us (2%)
    pallas_call x1, Pallas kernels, on_device(): pl.pallas_call(kernel, out_shape=[jax.ShapeDtypeStruct((1024, 128), F32)]...  56.5 us
    select_n x1, other arithmetic, on_device(): row, col = (jnp.where(lengths[0] > 0, t, 0.0) for t in (row, col))  2.24 us

profile of v3, /device:TPU:1, one launch (start us, length us, event | category | flops | bytes accessed | tf_op | source)
XLA Modules:
  0.0 60.0 jit_solution(5955434823419307181)
XLA Ops:
  1.3 56.5 %shard_map.86 = (f32[1024,128]{1,0:T(8,128)}, f32[1024,128]{1,0:T(8,128)}) custom-call(bf16[1,1024,8192]{2,1,0:T(8,128)(2,1)} %front_ref.1, bf16[1,1024,256]{2,1,0:T(8,128)(2,1)} %omega_ref.1, bf16[1,1024,256]{2,1,0:T(8,128)(2,1)} %psi_ref.1, s32[1]{0:T(128)S(6)} %copy.11.length_in, s32[1,8]{1,0:T(1,128)} %chosen_in.1, s32[16]{0:T(128)} %bitcast.14, ...), custom_call_target="tpu_custom_call" | custom-call | flops 8999999488 | bytes 20000000 | tf_op jit(solution)/shard_map/pallas_call | solution.py:493
  57.8 2.2 %broadcast_select_fusion = (f32[1024,128]{1,0:T(8,128)}, f32[1024,128]{1,0:T(8,128)}) fusion(f32[1024,128]{1,0:T(8,128)} %get-tuple-element.5, pred[]{:T(512)} %bitcast, f32[1024,128]{1,0:T(8,128)} %get-tuple-element.4), kind=kLoop, calls=%fused_computation | loop fusion | flops 262144 | bytes 2097153 | tf_op jit(solution)/shard_map/jit(_where)/select_n | solution.py:537

commit v4 on v3

--- a/solution.py
+++ b/solution.py
@@ -77,15 +77,18 @@
     n = w.shape[0]
     o = blk * NB
     r8 = lax.broadcasted_iota(I32, (8, 128), 0)
-    wb = w[o : o + NB, :]
+    at = o // 128 * 128
+    span = slice(at, at + 384)
+    wb = w[o : o + NB, span]
     wide = wb.shape[1] // 128
     tile = lambda f: jnp.concatenate([f] * wide, axis=1)
     strips = [wb[8 * s : 8 * s + 8, :] for s in range(NB // 8)]
     for s in range(NB // 8):
         so = o + 8 * s
+        sa = so - at
         left = NB // 8 - s
         cols = [
-            [jnp.broadcast_to(strips[t][:, so + k : so + k + 1], (8, 128)) for k in range(8)]
+            [jnp.broadcast_to(strips[t][:, sa + k : sa + k + 1], (8, 128)) for k in range(8)]
             for t in range(s, NB // 8)
         ]
         st = strips[s]
@@ -110,11 +113,11 @@
                 acc = acc - tile(fs[t][k]) * jnp.broadcast_to(st[k : k + 1, :], st.shape)
             strips[s + t] = acc
         strips[s] = st
-        w[so : so + 8, :] = st * tile(scale)
+        w[so : so + 8, span] = st * tile(scale)
     if o + NB < n:
-        y = w[o : o + NB, :]
-        later = y[:, o + NB : n]
-        w[o + NB : n, :] = w[o + NB : n, :] - lax.dot_general(
+        y = w[o : o + NB, span]
+        later = w[o : o + NB, o + NB : n]
+        w[o + NB : n, span] = w[o + NB : n, span] - lax.dot_general(
             later, y, (((0,), (0,)), ((), ())), precision=HI, preferred_element_type=F32
         )
 
@@ -415,8 +418,8 @@
         ring_send(L2 + g, left)
         ring_send(L3 + g, left)
 
+    cross_third(1)
     ring_middle(0)
-    cross_third(1)
     wait_cross(1, near_second)
     row_adds(1, both(near_second) + [(2, c, 0), (2, c, 1)])
     wait_cross(1, ((2, 0), (2, 1)))
@@ -443,14 +446,13 @@
 
     weights = [[jnp.where(assign_ref[ch] == p, 1.0, 0.0).astype(F32) for p in range(4)] for ch in range(16)]
 
-    def gather(mat, g):
+    def gather(mat, g, after=None):
         for cp in placed[mat, g]:
             cp.wait_recv()
         out = (row_ref, col_ref)[mat]
 
-        @pl.loop(0, 2)
-        def _(t):
-            at = pl.ds(pl.multiple_of(t * 32, 32), 32)
+        def add_tile(t):
+            at = pl.ds(t * 32 if after else pl.multiple_of(t * 32, 32), 32)
             acc = [[jnp.zeros((32, 128), F32) for _ in range(2)] for _ in range(4)]
             for ch in range(16):
                 q = arrived[mat, g, ch, at, :]
@@ -463,6 +465,13 @@
                 for h in range(2):
                     out[pl.ds(h * 512 + t * 256 + g * 4 + p, 32, stride=8), :] = acc[p][h]
 
+        if after is None:
+            pl.loop(0, 2)(add_tile)
+        else:
+            for t in range(2):
+                add_tile(t)
+                after(t)
+
     gather(0, 0)
     finish_columns(0)
     gather(0, 1)
@@ -470,16 +479,24 @@
     row_done.start()
     finish_columns(1)
     gather(1, 0)
-    gather(1, 1)
-    col_done = pltpu.make_async_copy(col_ref, col_out, insem.at[4])
-    col_done.start()
+    col_done = []
+
+    def send_columns(t):
+        for h in range(2):
+            at = pl.ds(h * 512 + t * 256, 256)
+            cp = pltpu.make_async_copy(col_ref.at[at], col_out.at[at], insem.at[8 + t * 2 + h])
+            cp.start()
+            col_done.append(cp)
+
+    gather(1, 1, send_columns)
 
     for cp in sent:
         cp.wait_send()
     for dx in range(4):
         partial_to_partner(dx).wait_send()
     row_done.wait()
-    col_done.wait()
+    for cp in col_done:
+        cp.wait()
 
 
 def panel_of(t):
@@ -519,7 +536,7 @@
             pltpu.VMEM((2, 2, 16, 65, 128), I32),
             pltpu.VMEM((2, 2, 16, 65, 128), I32),
             dma((8,)),
-            dma((8,)),
+            dma((12,)),
             dma((2, 14)),
             dma((2, 14)),
             dma((4,)),

time: 60.7 us -> 60.1 us (level)
  no operation moved by 1% of the time
where the time goes in v4:
time: 60.1 us; the launch traced here: 59.8 us
  Pallas kernels  56.2 us (94%)
  other arithmetic  2.24 us (4%)
  between operations  1.29 us (2%)
    pallas_call x1, Pallas kernels, on_device(): pl.pallas_call(kernel, out_shape=[jax.ShapeDtypeStruct((1024, 128), F32)]...  56.2 us
    select_n x1, other arithmetic, on_device(): row, col = (jnp.where(lengths[0] > 0, t, 0.0) for t in (row, col))  2.24 us

profile of v4, /device:TPU:1, one launch (start us, length us, event | category | flops | bytes accessed | tf_op | source)
XLA Modules:
  0.0 59.8 jit_solution(12341786303074219964)
XLA Ops:
  1.3 56.2 %shard_map.86 = (f32[1024,128]{1,0:T(8,128)}, f32[1024,128]{1,0:T(8,128)}) custom-call(bf16[1,1024,8192]{2,1,0:T(8,128)(2,1)} %front_ref.1, bf16[1,1024,256]{2,1,0:T(8,128)(2,1)} %omega_ref.1, bf16[1,1024,256]{2,1,0:T(8,128)(2,1)} %psi_ref.1, s32[1]{0:T(128)S(6)} %copy.11.length_in, s32[1,8]{1,0:T(1,128)} %chosen_in.1, s32[16]{0:T(128)} %bitcast.14, ...), custom_call_target="tpu_custom_call" | custom-call | flops 8999999488 | bytes 20000000 | tf_op jit(solution)/shard_map/pallas_call | solution.py:510
  57.5 2.2 %broadcast_select_fusion = (f32[1024,128]{1,0:T(8,128)}, f32[1024,128]{1,0:T(8,128)}) fusion(f32[1024,128]{1,0:T(8,128)} %get-tuple-element.5, pred[]{:T(512)} %bitcast, f32[1024,128]{1,0:T(8,128)} %get-tuple-element.4), kind=kLoop, calls=%fused_computation | loop fusion | flops 262144 | bytes 2097153 | tf_op jit(solution)/shard_map/jit(_where)/select_n | solution.py:554
